TPU v7x, 512 devices: a whole 4x4x16 slice. The times are simulated.
512 devices in a mesh: seq: 128 (over y, x_hi, z), scene: 4 (over x_lo, core).
Axes of the slice: x: 4 (x_hi: 2, x_lo: 2; x = x_hi * 2 + x_lo), y: 4, z: 16, core: 2. Of those that a mesh axis runs over, the one named last changes fastest.
Arguments:
- features: bfloat16 [131072, 1280], P(('scene', 'seq')), parts along dimension 0, may hold values from -6 to 6
- norm_gain: float32 [1280], replicated, may hold values from 0.1 to 1.9
- pred_weight: bfloat16 [1280, 1024], replicated, may hold values from -0.15625 to 0.15625
- target: bfloat16 [131072, 1024], P(('scene', 'seq')), parts along dimension 0, may hold values from -6 to 6
- patch_mask: int32 [131072], P(('scene', 'seq')), parts along dimension 0, may hold values 0 or 1
- band_level: int32 [16], replicated, may hold values from 1 to 16
Outputs:
- pixel_grad: float32 [131072, 1024], P(('scene', 'seq')), parts along dimension 0
- loss: float32 [4], P('scene'), parts along dimension 0
There are 4 independent parts, one for each index of `scene`. A program takes and returns all parts, laid end to end along the dimension named above; an argument that names none is the same for every part. Nothing has to cross between parts.
All inputs are finite; a program needn't handle non-finite values. No bound on the sum of `patch_mask` on one device may be relied on, other than what follows from the above.
Results may differ from a plain program's by a relative error of at most 0.0017.
The roundings to bfloat16 on the way count: a program that leaves them out, or rounds other values in their place, can miss the bound.
Values sent between devices are 32-bit elements; how exact they have to be, the bound alone decides.
A program may use at most 64 MiB of HBM per device.

v0:
```python
import math

import jax
import jax.numpy as jnp
from jax import lax
from jax.sharding import PartitionSpec as P

PATCH = 16
CH = 4
W = 4096
NBIN = 16
PIX = 1024
PC = 256


highest = lax.Precision.HIGHEST


def make_table(count_left, count_right, modulus, rotation):
    product = (
        jnp.arange(count_left, dtype=jnp.int32)[:, None]
        * jnp.arange(count_right, dtype=jnp.int32)[None, :]
        % modulus
    )
    phase_angle = product.astype(jnp.float32) * (2.0 * math.pi / modulus)
    return (jnp.cos(phase_angle), rotation * jnp.sin(phase_angle))


def complex_form(cos_table, sin_table):
    return jnp.stack((jnp.stack((cos_table, -sin_table)), jnp.stack((sin_table, cos_table))))


def split_length(length):
    inner_size = math.gcd(length, 128)
    return (length // inner_size, inner_size)


def true_frequency(position, length):
    outer_size, inner_size = split_length(length)
    return position // inner_size + outer_size * (position % inner_size)


def forward(real_part, imag_part):
    row_total, length = real_part.shape
    outer_size, inner_size = split_length(length)
    outer_form = complex_form(*make_table(outer_size, outer_size, outer_size, -1.0))
    twist_r, twist_i = make_table(outer_size, inner_size, length, -1.0)
    inner_form = complex_form(*make_table(inner_size, inner_size, inner_size, -1.0))
    if imag_part is None:
        blocks = real_part.reshape(row_total, outer_size, inner_size)
        section = jnp.einsum("ckn,bnm->cbkm", outer_form[:, 0], blocks, precision=highest)
    else:
        blocks = jnp.stack((real_part, imag_part)).reshape(2, row_total, outer_size, inner_size)
        section = jnp.einsum("cdkn,dbnm->cbkm", outer_form, blocks, precision=highest)
    turned = jnp.stack(
        (section[0] * twist_r - section[1] * twist_i, section[0] * twist_i + section[1] * twist_r)
    )
    final = jnp.einsum("cdmj,dbkm->cbkj", inner_form, turned, precision=highest)
    return (final[0].reshape(row_total, length), final[1].reshape(row_total, length))


def backward(real_part, imag_part):
    row_total, length = real_part.shape
    outer_size, inner_size = split_length(length)
    outer_form = complex_form(*make_table(outer_size, outer_size, outer_size, 1.0))
    twist_r, twist_i = make_table(outer_size, inner_size, length, 1.0)
    inner_form = complex_form(*make_table(inner_size, inner_size, inner_size, 1.0))
    blocks = jnp.stack((real_part, imag_part)).reshape(2, row_total, outer_size, inner_size)
    section = jnp.einsum("cdjm,dbkj->cbkm", inner_form, blocks, precision=highest)
    turned = jnp.stack(
        (section[0] * twist_r - section[1] * twist_i, section[0] * twist_i + section[1] * twist_r)
    )
    final = jnp.einsum("cdnk,dbkm->cbnm", outer_form, turned, precision=highest)
    return (final[0].reshape(row_total, length), final[1].reshape(row_total, length))


def square_weights(band_level, start, col_total, length_y, length_x):
    col_index = true_frequency(start + jnp.arange(col_total, dtype=jnp.int32), length_x)
    row_index = true_frequency(jnp.arange(length_y, dtype=jnp.int32), length_y)
    fold_x = jnp.where(col_index < length_x // 2, col_index, length_x - col_index)
    fold_y = jnp.where(row_index < length_y // 2, row_index, length_y - row_index)
    band_x = fold_x * NBIN // (length_x // 2)
    band_y = fold_y * NBIN // (length_y // 2)
    band_index = jnp.minimum(jnp.maximum(band_x[:, None], band_y[None, :]), NBIN - 1)
    level_values = band_level.astype(jnp.float32)
    weights = jnp.zeros(band_index.shape, jnp.float32)
    for level in range(NBIN):
        weights = weights + jnp.where(band_index == level, level_values[level], 0.0)
    return weights / 8.0


def shards(features, norm_gain, pred_weight, target, patch_mask, band_level):
    seq_total = lax.axis_size("seq")
    tok_total = features.shape[0]
    values = features.astype(jnp.float32)
    centre = values - jnp.mean(values, axis=-1, keepdims=True)
    spread = jnp.mean(centre * centre, axis=-1, keepdims=True)
    normed = (centre * lax.rsqrt(spread + 1e-06) * norm_gain).astype(jnp.bfloat16)
    predicted = jnp.dot(normed, pred_weight, preferred_element_type=jnp.float32)
    keep_mask = patch_mask.astype(jnp.float32)[:, None]
    residue = (predicted - target.astype(jnp.float32)) * keep_mask
    band_rows = tok_total // PC * PATCH
    image = (
        residue.reshape(band_rows // PATCH, PC, PATCH, PATCH, CH)
        .transpose(4, 0, 2, 1, 3)
        .reshape(CH, band_rows, W)
    )
    col_width = W // seq_total
    full_rows = band_rows * seq_total
    grad_scale = 2.0 / (full_rows * W)
    item_total = CH
    plane_r = image.reshape(item_total * band_rows, W)
    spec_r, spec_i = forward(plane_r, None)

    def to_send(part):
        return (
            part.reshape(item_total, band_rows, seq_total, col_width)
            .transpose(0, 2, 3, 1)
            .reshape(item_total, seq_total, col_width * band_rows)
        )

    weights = square_weights(band_level, lax.axis_index("seq") * col_width, col_width, full_rows, W)
    recv_r = lax.all_to_all(to_send(spec_r), "seq", split_axis=1, concat_axis=1, tiled=True)
    recv_i = lax.all_to_all(to_send(spec_i), "seq", split_axis=1, concat_axis=1, tiled=True)
    item_count = recv_r.shape[0]

    def columns(part):
        return (
            part.reshape(item_count, seq_total, col_width, band_rows)
            .transpose(0, 2, 1, 3)
            .reshape(item_count * col_width, full_rows)
        )

    freq_r, freq_i = forward(columns(recv_r), columns(recv_i))
    freq_r = freq_r.reshape(item_count, col_width, full_rows)
    freq_i = freq_i.reshape(item_count, col_width, full_rows)
    spectral_power = jnp.sum(weights * (freq_r * freq_r + freq_i * freq_i), axis=(1, 2)).reshape(
        item_count, 1
    )
    back_r, back_i = backward(
        (weights * freq_r).reshape(item_count * col_width, full_rows),
        (weights * freq_i).reshape(item_count * col_width, full_rows),
    )

    def rows_back(part):
        return (
            part.reshape(item_count, col_width, seq_total, band_rows)
            .transpose(0, 2, 1, 3)
            .reshape(item_count, seq_total, col_width * band_rows)
        )

    home_r = lax.all_to_all(rows_back(back_r), "seq", split_axis=1, concat_axis=1, tiled=True)
    home_i = lax.all_to_all(rows_back(back_i), "seq", split_axis=1, concat_axis=1, tiled=True)
    home_r, home_i, spectral_power = (home_r, home_i, spectral_power)

    def rows_again(part):
        return (
            part.reshape(item_total, seq_total, col_width, band_rows)
            .transpose(0, 3, 1, 2)
            .reshape(item_total * band_rows, W)
        )

    grid_r, grid_i = backward(rows_again(home_r), rows_again(home_i))
    grad_image = grid_r.reshape(CH, band_rows, W) * grad_scale
    total = lax.psum(jnp.sum(spectral_power), "seq")
    loss = (total / (full_rows * W) / (CH * full_rows * W)).reshape(1)
    pixel_grad = (
        grad_image.reshape(CH, band_rows // PATCH, PATCH, PC, PATCH)
        .transpose(1, 3, 2, 4, 0)
        .reshape(tok_total, PIX)
        * keep_mask
    )
    return (pixel_grad, loss)


def solution(mesh):
    in_specs = (
        P(("scene", "seq"), None),
        P(),
        P(),
        P(("scene", "seq"), None),
        P(("scene", "seq")),
        P(),
    )
    out_specs = (P(("scene", "seq"), None), P("scene"))
    return jax.shard_map(shards, mesh=mesh, in_specs=in_specs, out_specs=out_specs, check_vma=False)
```

profile of v0, /device:TPU:2, one launch (start us, length us, event | category | flops | bytes accessed | tf_op | source)
XLA Modules:
  0.0 724.0 jit_solution(12037504153148739151)
XLA Ops:
  1.8 1.3 convert_reduce_fusion
  3.1 1.4 fusion.33
  4.5 0.7 convert_element_type.200
  5.2 3.1 fusion.32
  8.3 1.6 copy.37
  9.9 0.3 reshape.645
  10.2 4.6 copy.38
  14.8 6.5 reshape.656
  21.2 3.0 convolution_bitcast_fusion
  24.6 1.8 fusion.23
  26.4 1.5 fusion.148
  28.0 3.7 reshape_reshape_squeeze.16
  31.7 2.9 copy.44
  34.6 1.4 copy.45
  36.0 22.1 %all-to-all-start.1 = ((f32[4,128,512]{2,0,1:T(4,128)}), f32[4,128,512]{2,0,1:T(4,128)S(1)}, u32[]{:S(2)}, u32[]{:S(2)}) async-start(f32[4,128,512]{2,0,1:T(4,128)} %copy.45), calls=%async_computation.1 | async-start | bytes 2097152 | tf_op jit(solution)/shard_map/all_to_all | solution.py:124
  58.1 2.4 reshape_reshape_squeeze.15
  60.5 2.9 copy.40
  63.4 1.4 copy.41
  64.8 47.3 %all-to-all-done.1 = f32[4,128,512]{2,0,1:T(4,128)S(1)} async-done(((f32[4,128,512]{2,0,1:T(4,128)}), f32[4,128,512]{2,0,1:T(4,128)S(1)}, u32[]{:S(2)}, u32[]{:S(2)}) %all-to-all-start.1) | async-done | bytes 1048608 | tf_op jit(solution)/shard_map/all_to_all | solution.py:124
  112.1 10.7 %all-to-all-start = ((f32[4,128,512]{2,0,1:T(4,128)}), f32[4,128,512]{2,0,1:T(4,128)}, u32[]{:S(2)}, u32[]{:S(2)}) async-start(f32[4,128,512]{2,0,1:T(4,128)} %copy.41), calls=%async_computation | async-start | bytes 2097152 | tf_op jit(solution)/shard_map/all_to_all | solution.py:123
  122.8 0.7 fusion.149
  123.6 10.6 %add_multiply_fusion = f32[32,2048]{1,0:T(8,128)S(1)} fusion(f32[]{:T(128)} %bitcast.15, f32[]{:T(128)} %bitcast.14, f32[]{:T(128)} %bitcast.13, f32[]{:T(128)} %bitcast.12, f32[]{:T(128)} %bitcast.11, f32[]{:T(128)} %bitcast.10, f32[]{:T(128)} %bitcast.9, f32[]{:T(128)} %bitcast.8, f32[]{:T(128)} %bitcast.7, f32[]{:T(128)} %bitcast.6, f32[]{:T(128)} %bitcast.5, ...), kind=kLoop, calls=%fused_computation.62 | loop fusion | flops 3276800 | bytes 270528 | tf_op jit(solution)/shard_map/div | solution.py:89
  134.3 1.2 copy.87
  135.8 0.4 copy.46
  136.2 4.5 copy.47
  140.7 3.7 stack.181
  144.4 1.4 copy.49
  145.8 31.0 %all-to-all-done = f32[4,128,512]{2,0,1:T(4,128)} async-done(((f32[4,128,512]{2,0,1:T(4,128)}), f32[4,128,512]{2,0,1:T(4,128)}, u32[]{:S(2)}, u32[]{:S(2)}) %all-to-all-start) | async-done | bytes 1048608 | tf_op jit(solution)/shard_map/all_to_all | solution.py:123
  176.7 1.6 copy.42
  178.3 4.5 copy.43
  182.8 3.9 stack.180
  186.7 1.4 copy.48
  188.1 3.4 fusion.22
  191.9 2.9 fusion.27
  194.8 1.2 multiply_reduce_fusion
  196.3 3.1 fusion.24
  199.6 1.9 fusion.21
  201.5 1.5 fusion.147
  203.0 1.8 copy.59
  204.8 3.2 reshape_reshape_squeeze.18
  208.0 3.9 copy.60
  211.9 1.4 copy.61
  213.4 9.5 %all-to-all-start.3 = ((f32[4,128,512]{2,0,1:T(4,128)}), f32[4,128,512]{2,0,1:T(4,128)S(1)}, u32[]{:S(2)}, u32[]{:S(2)}) async-start(f32[4,128,512]{2,0,1:T(4,128)} %copy.61), calls=%async_computation.3 | async-start | bytes 2097152 | tf_op jit(solution)/shard_map/all_to_all | solution.py:153
  222.9 1.6 copy.54
  224.5 3.2 reshape_reshape_squeeze.17
  227.6 3.9 copy.55
  231.6 1.4 copy.56
  233.0 44.3 %all-to-all-done.3 = f32[4,128,512]{2,0,1:T(4,128)S(1)} async-done(((f32[4,128,512]{2,0,1:T(4,128)}), f32[4,128,512]{2,0,1:T(4,128)S(1)}, u32[]{:S(2)}, u32[]{:S(2)}) %all-to-all-start.3) | async-done | bytes 1048608 | tf_op jit(solution)/shard_map/all_to_all | solution.py:153
  277.3 10.0 %all-to-all-start.2 = ((f32[4,128,512]{2,0,1:T(4,128)}), f32[4,128,512]{2,0,1:T(4,128)}, u32[]{:S(2)}, u32[]{:S(2)}) async-start(f32[4,128,512]{2,0,1:T(4,128)} %copy.56), calls=%async_computation.2 | async-start | bytes 2097152 | tf_op jit(solution)/shard_map/all_to_all | solution.py:152
  287.4 392.7 %psum.7 = f32[]{:T(128)} all-reduce(f32[]{:T(128)} %get-tuple-element.2), channel_id=1, replica_groups=mesh['seq'=128,'scene'=4] {'seq'}, use_global_device_ids=true, to_apply=%region_3.4 | all-reduce | flops 1 | bytes 8 | tf_op jit(solution)/shard_map/psum | solution.py:165
  680.7 0.4 copy.62
  681.1 2.7 copy.63
  683.8 4.1 stack.202
  687.9 1.6 copy.57
  689.5 2.7 copy.58
  692.1 4.1 stack.201
  696.2 3.3 fusion.20
  699.9 1.9 fusion.19
  701.8 1.1 slice_multiply_fusion
  702.9 5.9 mul.1009
  708.8 6.0 copy.66
  714.8 2.7 reshape.654
  717.6 2.5 copy.67
  720.1 2.3 broadcast_multiply_fusion
  (39 shorter events, 3.2 us)
Async XLA Ops:
  0.6 4.6 copy-start
  36.0 22.1 %copy-start.2 = (f32[1,64,32,128]{3,2,0,1:T(8,128)S(1)}, f32[1,64,32,128]{3,2,0,1:T(8,128)}, u32[]{:S(2)}) copy-start(f32[1,64,32,128]{3,2,0,1:T(8,128)} %get-tuple-element.15) | copy-start | bytes 3145732
  36.0 76.1 %all-to-all-start.1 = ((f32[4,128,512]{2,0,1:T(4,128)}), f32[4,128,512]{2,0,1:T(4,128)S(1)}, u32[]{:S(2)}, u32[]{:S(2)}) async-start(f32[4,128,512]{2,0,1:T(4,128)} %copy.45), calls=%async_computation.1 | async-start | bytes 2097152 | tf_op jit(solution)/shard_map/all_to_all | solution.py:124
  63.4 59.4 %copy-start.4 = (s32[16]{0:T(128)S(1)}, s32[16]{0:T(128)}, u32[]{:S(2)}) copy-start(s32[16]{0:T(128)} %param.11) | copy-start | bytes 196
  112.1 64.6 %all-to-all-start = ((f32[4,128,512]{2,0,1:T(4,128)}), f32[4,128,512]{2,0,1:T(4,128)}, u32[]{:S(2)}, u32[]{:S(2)}) async-start(f32[4,128,512]{2,0,1:T(4,128)} %copy.41), calls=%async_computation | async-start | bytes 2097152 | tf_op jit(solution)/shard_map/all_to_all | solution.py:123
  191.9 2.9 copy-start.3
  213.4 63.9 %all-to-all-start.3 = ((f32[4,128,512]{2,0,1:T(4,128)}), f32[4,128,512]{2,0,1:T(4,128)S(1)}, u32[]{:S(2)}, u32[]{:S(2)}) async-start(f32[4,128,512]{2,0,1:T(4,128)} %copy.61), calls=%async_computation.3 | async-start | bytes 2097152 | tf_op jit(solution)/shard_map/all_to_all | solution.py:153
  277.3 410.6 %all-to-all-start.2 = ((f32[4,128,512]{2,0,1:T(4,128)}), f32[4,128,512]{2,0,1:T(4,128)}, u32[]{:S(2)}, u32[]{:S(2)}) async-start(f32[4,128,512]{2,0,1:T(4,128)} %copy.56), calls=%async_computation.2 | async-start | bytes 2097152 | tf_op jit(solution)/shard_map/all_to_all | solution.py:152
  714.8 7.6 %copy-start.1 = (bf16[1280,1024]{1,0:T(8,128)(2,1)S(1)}, bf16[1280,1024]{1,0:T(8,128)(2,1)}, u32[]{:S(2)}) copy-start(bf16[1280,1024]{1,0:T(8,128)(2,1)} %param.8) | copy-start | bytes 7864324
where the time goes:
time: 733 us; the launch traced here: 724 us
  blocking collectives  393 us (54%)
  waiting for transfers between devices  123 us (17%)
  local copies, waits for them, and re-layouts  107 us (15%)
  starting transfers between devices  52.3 us (7%)
  matrix products  24.5 us (3%)
  other arithmetic  21.7 us (3%)
    psum x1, blocking collectives, shards(): total = lax.psum(jnp.sum(spectral_power), 'seq')  393 us
    all_to_all x1, waiting for transfers between devices, shards(): lax.all_to_all(to_send(spec_i), 'seq', split_axis=1, concat_axis=1, tiled...  47.3 us
    all_to_all x1, waiting for transfers between devices, shards(): lax.all_to_all(rows_back(back_i), 'seq', split_axis=1, concat_axis=1, til...  44.3 us
    all_to_all x1, waiting for transfers between devices, shards(): lax.all_to_all(to_send(spec_r), 'seq', split_axis=1, concat_axis=1, tiled...  31 us
    all_to_all x1, starting transfers between devices, shards(): lax.all_to_all(to_send(spec_i), 'seq', split_axis=1, concat_axis=1, tiled...  22.1 us
  transfers between devices with their start and end apart: 4, of which 3 were waited for; matrix products, arithmetic and copies ran while one was open for 6% of the time, Pallas kernels for 0%

commit v1 on v0

v1 whole, which is shorter than its diff:
```python
import math

import jax
import jax.numpy as jnp
import numpy as np
import ml_dtypes
from jax import lax
from jax.experimental import pallas as pl
from jax.experimental.pallas import tpu as pltpu
from jax.sharding import PartitionSpec as P

D = 1280
PIX = 1024
TOK = 256
NBIN = 16
N = 128
ZR = 16
QR = 8
MESH = pl.DeviceIdType.MESH
F32 = jnp.float32
BF16 = jnp.bfloat16


def halves(table):
    high = table.astype(ml_dtypes.bfloat16)
    low = (table - high.astype(np.float64)).astype(ml_dtypes.bfloat16)
    return high, low


def lane_of(channel, k2, part):
    return (channel % 2) * 64 + k2 * 4 + (channel // 2) * 2 + part


def token_table():
    t = np.arange(TOK)
    k = np.arange(128)
    angle = 2 * np.pi * np.outer(k, t) / TOK
    top = np.cos(angle) * math.sqrt(2 / TOK)
    low = np.sin(angle) * math.sqrt(2 / TOK)
    top[0] = 1 / math.sqrt(TOK)
    low[0] = (1 - 2 * (t % 2)) / math.sqrt(TOK)
    return np.concatenate([top, low])


def pixel_tables():
    plain = np.zeros((256, 256))
    first = np.zeros((256, 256))
    for pair in range(2):
        for x in range(16):
            for c in range(4):
                a = pair * 64 + x * 4 + c
                b = 128 + a
                for k2 in range(16):
                    re = pair * 128 + lane_of(c, k2, 0)
                    im = pair * 128 + lane_of(c, k2, 1)
                    phi = 2 * math.pi * x * k2 / 16
                    plain[a, re] = math.cos(phi) / 4
                    plain[a, im] = math.sin(phi) / 4
                    plain[b, re] = -math.sin(phi) / 4
                    plain[b, im] = math.cos(phi) / 4
                    if k2 == 0:
                        first[a, re] = 1 / 4
                        first[a, im] = (1 - 2 * (x % 2)) / 4
                    elif k2 < 8:
                        first[a, re] = math.cos(phi) * math.sqrt(2) / 4
                        first[a, im] = math.sin(phi) * math.sqrt(2) / 4
                    else:
                        psi = 2 * math.pi * x * (k2 + 0.5) / 16
                        first[b, re] = math.cos(psi) * math.sqrt(2) / 4
                        first[b, im] = math.sin(psi) * math.sqrt(2) / 4
    return plain, first


def pixel_turn():
    lane = np.arange(128)
    x = (lane % 64) // 4
    angle = 2 * np.pi * np.outer(np.arange(128), x) / 4096
    return np.cos(angle).astype(np.float32), np.sin(angle).astype(np.float32)


def row_tables():
    k = np.arange(128)
    angle = 2 * np.pi * (np.outer(k, k) % 128) / 128
    outer = np.concatenate([np.cos(angle), np.sin(angle)]) / math.sqrt(128)
    s = np.arange(16)
    angle = 2 * np.pi * (np.outer(s, s) % 16) / 16
    eye = np.eye(8)
    inner = np.concatenate([np.kron(np.cos(angle), eye), np.kron(np.sin(angle), eye)]) / 4
    angle = 2 * np.pi * np.outer(s, k) / 2048
    wide = np.broadcast_to(angle[:, :, None], (16, 128, 128))
    return outer, inner, np.cos(wide).astype(np.float32), np.sin(wide).astype(np.float32)


def doubled(table):
    high, low = halves(table)
    return np.concatenate([high, high], axis=1), low


def split(x):
    high = x.astype(BF16)
    return high, (x - high.astype(F32)).astype(BF16)


def mm(a, b, dims=((1,), (0,))):
    return lax.dot_general(a, b, (dims, ((), ())), preferred_element_type=F32)


def times(x, high, low, dims=((1,), (0,))):
    xh, xl = split(x)
    return mm(xh, high, dims) + (mm(xl, high, dims) + mm(xh, low, dims))


def left(high, low, x, dims=((1,), (0,))):
    xh, xl = split(x)
    return mm(high, xh, dims) + (mm(high, xl, dims) + mm(low, xh, dims))


def stacked(double, low, x):
    xh, xl = split(x)
    return mm(double, jnp.concatenate([xh, xl], axis=0)) + mm(low, xh)


def kernel(
    feat, gain, head, targ, mask, level,
    t_hi, t_lo, m_hi, m_lo, s_hi, s_lo, xc, xs, fa_hi, fa_lo, fb_hi, fb_lo, ca, sa,
    out, loss,
    normed, tm_hi, tm_lo, s0, s1, r0, r1, y0, y1, z0, z1, u, wt, part1, part2,
    fsend, frecv, bsend, brecv, lsend, lrecv,
):
    me = lax.axis_index("seq")
    mz = lax.rem(me, ZR)
    mq = me // ZR
    sends, recvs, backs, homes = (s0, s1), (r0, r1), (y0, y1), (z0, z1)

    barrier = pltpu.get_barrier_semaphore()

    @pl.loop(1, N)
    def _(p):
        pl.semaphore_signal(barrier, inc=1, device_id={"seq": lax.rem(me + p, N)}, device_id_type=MESH)

    for row in range(0, TOK, 64):
        values = feat[row : row + 64, :].astype(F32)
        centre = values - jnp.mean(values, axis=-1, keepdims=True)
        spread = jnp.mean(centre * centre, axis=-1, keepdims=True)
        normed[row : row + 64, :] = (centre * lax.rsqrt(spread + 1e-06) * gain[...]).astype(BF16)

    keep = mask[...].astype(F32)
    tm_hi[...] = (t_hi[...].astype(F32) * keep).astype(BF16)
    tm_lo[...] = (t_lo[...].astype(F32) * keep).astype(BF16)

    def scatter(src, dst, send, recv):
        @pl.loop(1, N)
        def _(p):
            t = lax.rem(me + p, N)
            pltpu.make_async_remote_copy(
                src_ref=src.at[pl.ds(pl.multiple_of(t * 8, 8), 8)],
                dst_ref=dst.at[pl.ds(pl.multiple_of(me * 8, 8), 8)],
                send_sem=send,
                recv_sem=recv,
                device_id={"seq": t},
                device_id_type=MESH,
            ).start()

    def await_all(ref, sem):
        whole = ref.at[pl.ds(0, (N - 1) * 8)]
        pltpu.make_async_copy(whole, whole, sem).wait()

    mine = pl.ds(pl.multiple_of(me * 8, 8), 8)

    for h in range(2):
        for g in range(2):
            lo = h * 512 + g * 256
            error = mm(normed[...], head[:, lo : lo + 256]) - targ[:, lo : lo + 256].astype(F32)
            ab = left(tm_hi[...], tm_lo[...], error)
            for pr in range(2):
                r = g * 4 + pr * 2
                a = ab[:128, pr * 128 : pr * 128 + 128]
                b = ab[128:, pr * 128 : pr * 128 + 128]
                a, b = a * xc[...] - b * xs[...], b * xc[...] + a * xs[...]
                both = jnp.concatenate([a, b], axis=1)
                spec = times(both, m_hi[...], m_lo[...])
                first = times(both[:8], s_hi[...], s_lo[...])
                for i in range(2):
                    sends[h][pl.ds(r + i, 128, stride=8), :] = spec[:, i * 128 : i * 128 + 128]
                    sends[h][r + i : r + i + 1, :] = first[:1, i * 128 : i * 128 + 128]
        recvs[h][mine, :] = sends[h][mine, :]
        if h == 0:
            pl.semaphore_wait(barrier, N - 1)
        scatter(sends[h], recvs[h], fsend.at[h], frecv.at[h])

    lane = lax.broadcasted_iota(jnp.int32, (128, 128), 1)
    row = lax.broadcasted_iota(jnp.int32, (128, 128), 0)
    k2 = lax.shift_right_logical(lane, 2) & 15
    band_x = jnp.where(k2 < 8, 2 * k2, 31 - 2 * k2)
    band_x = jnp.where((lane & 1) + k2 * 2 + me * 64 == 1, NBIN - 1, band_x)
    sign = jnp.where(lane < 64, 1.0, -1.0).astype(F32)

    @pl.loop(0, 16)
    def _(jb):
        ky = jb * 8 + (row & 7) + lax.shift_right_logical(row, 3) * 128
        band_y = lax.shift_right_logical(jnp.minimum(ky, 2048 - ky), 6)
        band = jnp.minimum(jnp.maximum(band_y, band_x), NBIN - 1)
        value = jnp.zeros((128, 128), F32)
        for i in range(NBIN):
            value = jnp.where(band == i, level[i].astype(F32), value)
        wt[jb] = value * 0.125

    def swap(x):
        return pltpu.roll(x, 64, 1) * sign[: x.shape[0]]

    for h in range(2):
        await_all(recvs[h], frecv.at[h])
        for r in range(0, 8, 2):
            x = jnp.concatenate([recvs[h][pl.ds(r + i, 128, stride=8), :] for i in range(2)], axis=1)
            pq = stacked(fa_hi[...], fa_lo[...], x)
            for i in range(2):
                p = pq[:128, i * 128 : i * 128 + 128]
                q = pq[128:, i * 128 : i * 128 + 128]
                c, s = ca[h * 8 + r + i], sa[h * 8 + r + i]
                u[h * 8 + r + i] = (c * p - s * q) + swap(c * q + s * p)

    def middle(jb, acc):
        at = [pl.ds(pl.multiple_of(jb * 16 + i * 8, 8), 8) for i in range(2)]
        x = jnp.concatenate([u[:, at[i], :].reshape(128, 128) for i in range(2)], axis=1)
        pq = stacked(fb_hi[...], fb_lo[...], x)
        vs = []
        for i in range(2):
            v = pq[:128, i * 128 : i * 128 + 128] + swap(pq[128:, i * 128 : i * 128 + 128])
            wv = wt[jb * 2 + i] * v
            acc = acc + jnp.sum((wv * v).reshape(16, 8, 128), axis=0)
            vs.append(wv)
        pq = stacked(fb_hi[...], fb_lo[...], jnp.concatenate(vs, axis=1))
        for i in range(2):
            p = pq[:128, i * 128 : i * 128 + 128]
            q = pq[128:, i * 128 : i * 128 + 128]
            c, s = ca[:, at[i], :].reshape(128, 128), sa[:, at[i], :].reshape(128, 128)
            u[:, at[i], :] = ((c * p - s * q) - swap(c * q + s * p)).reshape(16, 8, 128)
        return acc

    acc = lax.fori_loop(0, 8, middle, jnp.zeros((8, 128), F32))

    part1[pl.ds(pl.multiple_of(mz * 8, 8), 8), :] = acc

    @pl.loop(1, ZR)
    def _(p):
        pltpu.make_async_remote_copy(
            src_ref=part1.at[pl.ds(pl.multiple_of(mz * 8, 8), 8)],
            dst_ref=part1.at[pl.ds(pl.multiple_of(mz * 8, 8), 8)],
            send_sem=lsend.at[0],
            recv_sem=lrecv.at[0],
            device_id={"seq": mq * ZR + lax.rem(mz + p, ZR)},
            device_id_type=MESH,
        ).start()

    for h in range(2):
        for r in range(0, 8, 2):
            x = jnp.concatenate([u[h * 8 + r + i] for i in range(2)], axis=1)
            pq = stacked(fa_hi[...], fa_lo[...], x)
            for i in range(2):
                p = pq[:128, i * 128 : i * 128 + 128]
                q = pq[128:, i * 128 : i * 128 + 128]
                backs[h][pl.ds(r + i, 128, stride=8), :] = p - swap(q)
        homes[h][mine, :] = backs[h][mine, :]
        scatter(backs[h], homes[h], bsend.at[h], brecv.at[h])

    near = part1.at[pl.ds(0, (ZR - 1) * 8)]
    pltpu.make_async_copy(near, near, lsend.at[0]).wait()
    pltpu.make_async_copy(near, near, lrecv.at[0]).wait()
    part2[pl.ds(pl.multiple_of(mq * 8, 8), 8), :] = jnp.sum(part1[...].reshape(ZR, 8, 128), axis=0)

    @pl.loop(1, QR)
    def _(p):
        pltpu.make_async_remote_copy(
            src_ref=part2.at[pl.ds(pl.multiple_of(mq * 8, 8), 8)],
            dst_ref=part2.at[pl.ds(pl.multiple_of(mq * 8, 8), 8)],
            send_sem=lsend.at[1],
            recv_sem=lrecv.at[1],
            device_id={"seq": lax.rem(mq + p, QR) * ZR + mz},
            device_id_type=MESH,
        ).start()

    for h in range(2):
        await_all(homes[h], brecv.at[h])
        for g in range(2):
            lo = h * 512 + g * 256
            blocks = []
            for pr in range(2):
                r = g * 4 + pr * 2
                x = jnp.concatenate([homes[h][pl.ds(r + i, 128, stride=8), :] for i in range(2)], axis=1)
                flip = ((1,), (1,))
                spec = times(x, m_hi[...], m_lo[...], flip)
                first = times(x[:8], s_hi[...], s_lo[...], flip)
                top = lax.broadcasted_iota(jnp.int32, (8, 256), 0)
                head8 = jnp.where(top == 0, jnp.broadcast_to(first[:1], (8, 256)), spec[:8])
                spec = jnp.concatenate([head8, spec[8:]], axis=0)
                a, b = spec[:, :128], spec[:, 128:]
                blocks.append(jnp.concatenate([a * xc[...] + b * xs[...], b * xc[...] - a * xs[...]], axis=0))
            grad = left(tm_hi[...], tm_lo[...], jnp.concatenate(blocks, axis=1), ((0,), (0,)))
            out[:, lo : lo + 256] = grad * 2.0

    far = part2.at[pl.ds(0, (QR - 1) * 8)]
    pltpu.make_async_copy(far, far, lsend.at[1]).wait()
    pltpu.make_async_copy(far, far, lrecv.at[1]).wait()
    loss[0] = jnp.sum(part2[...]) * (1.0 / 33554432.0)
    for h in range(2):
        await_all(sends[h], fsend.at[h])
        await_all(backs[h], bsend.at[h])


def shards(features, norm_gain, pred_weight, target, patch_mask, band_level):
    plain, first = pixel_tables()
    outer, inner, ca, sa = row_tables()
    tables = [
        *halves(token_table()), *halves(plain), *halves(first), *pixel_turn(),
        *doubled(outer), *doubled(inner), ca, sa,
    ]
    vmem = pl.BlockSpec(memory_space=pltpu.VMEM)
    smem = pl.BlockSpec(memory_space=pltpu.SMEM)
    dma = pltpu.SemaphoreType.DMA
    block = pltpu.VMEM((N * 8, 128), F32)
    grad, loss = pl.pallas_call(
        kernel,
        out_shape=(jax.ShapeDtypeStruct((TOK, PIX), F32), jax.ShapeDtypeStruct((1,), F32)),
        in_specs=[vmem] * 5 + [smem] + [vmem] * len(tables),
        out_specs=(vmem, smem),
        scratch_shapes=[
            pltpu.VMEM((TOK, D), BF16),
            pltpu.VMEM((TOK, TOK), BF16),
            pltpu.VMEM((TOK, TOK), BF16),
            *[block] * 8,
            pltpu.VMEM((16, 128, 128), F32),
            pltpu.VMEM((16, 128, 128), F32),
            pltpu.VMEM((ZR * 8, 128), F32),
            pltpu.VMEM((QR * 8, 128), F32),
            *[dma((2,))] * 6,
        ],
        compiler_params=pltpu.CompilerParams(
            collective_id=0, has_side_effects=True, vmem_limit_bytes=48 * 2**20
        ),
    )(
        features, norm_gain.reshape(1, D), pred_weight, target, patch_mask.reshape(1, TOK), band_level,
        *[jnp.asarray(table) for table in tables],
    )
    return grad, loss


def solution(mesh):
    in_specs = (
        P(("scene", "seq"), None),
        P(),
        P(),
        P(("scene", "seq"), None),
        P(("scene", "seq")),
        P(),
    )
    out_specs = (P(("scene", "seq"), None), P("scene"))
    return jax.shard_map(shards, mesh=mesh, in_specs=in_specs, out_specs=out_specs, check_vma=False)
```

time: 733 us -> 152 us (0.21)
  the two profiles are of different devices: /device:TPU:2 before, /device:TPU:1 now
where the time goes in v1:
time: 152 us; the launch traced here: 149 us
  Pallas kernels  129 us (85%)
  local copies, waits for them, and re-layouts  18.2 us (12%)
  between operations  2.47 us (2%)
    pallas_call x1, Pallas kernels, shards(): pl.pallas_call(kernel, out_shape=(jax.ShapeDtypeStruct((TOK, PIX), F32),...  129 us
    unnamed x37, local copies, waits for them, and re-layouts  17.5 us

profile of v1, /device:TPU:1, one launch (start us, length us, event | category | flops | bytes accessed | tf_op | source)
XLA Modules:
  0.0 149.3 jit_solution(11780562996055849607)
XLA Ops:
  0.6 0.7 reshape.10.gain
  1.3 0.0 copy-start
  1.3 1.2 copy-done
  2.6 0.0 copy-start.1
  2.6 1.2 copy-done.1
  3.8 0.0 copy-start.2
  3.8 1.1 copy-done.2
  4.9 0.0 copy-start.3
  4.9 1.0 copy-done.3
  5.9 0.0 copy-start.4
  5.9 0.9 copy-done.4
  6.8 0.0 copy-start.5
  6.8 0.9 copy-done.5
  7.7 0.0 copy-start.6
  7.7 0.9 copy-done.6
  8.6 0.0 copy-start.7
  8.6 0.9 copy-done.7
  9.5 0.0 copy-start.8
  9.5 0.9 copy-done.8
  10.4 0.0 copy-start.9
  10.4 0.9 copy-done.9
  11.3 0.0 copy-start.10
  11.3 0.9 copy-done.10
  12.2 0.0 copy-start.11
  12.2 0.9 copy-done.11
  13.1 0.0 copy-start.12
  13.2 0.8 copy-done.12
  14.0 0.0 copy-start.13
  14.0 0.8 copy-done.13
  14.8 0.0 copy-start.14
  14.8 0.8 copy-done.14
  15.7 0.0 copy-start.15
  15.7 0.8 copy-done.15
  16.5 0.0 copy-start.16
  16.5 0.7 copy-done.16
  17.2 0.0 copy-start.17
  17.2 0.7 copy-done.17
  17.8 128.7 %shard_map.203 = (f32[256,1024]{1,0:T(8,128)S(1)}, f32[1]{0:T(128)}) custom-call(bf16[256,1280]{1,0:T(8,128)(2,1)S(1)} %copy-done.2, f32[1,1280]{1,0:T(1,128)S(1)} %reshape.10.gain, bf16[1280,1024]{1,0:T(8,128)(2,1)} %head.1, bf16[256,1024]{1,0:T(8,128)(2,1)S(1)} %copy-done.3, s32[1,256]{1,0:T(1,128)S(1)} %bitcast.1, s32[16]{0:T(128)S(1)} %copy-done.17, ...), custom_call_target="tpu_custom_call" | custom-call | tf_op jit(solution)/shard_map/pallas_call | solution.py:321
  146.5 1.0 copy.24
Async XLA Ops:
  1.3 1.2 copy-start
  2.6 1.2 copy-start.1
  3.8 1.1 copy-start.2
  4.9 1.0 copy-start.3
  5.9 0.9 copy-start.4
  6.8 0.9 copy-start.5
  7.7 0.9 copy-start.6
  8.6 0.9 copy-start.7
  9.5 0.9 copy-start.8
  10.4 0.9 copy-start.9
  11.3 0.9 copy-start.10
  12.2 0.9 copy-start.11
  13.1 0.8 copy-start.12
  14.0 0.8 copy-start.13
  14.8 0.8 copy-start.14
  15.7 0.8 copy-start.15
  16.5 0.7 copy-start.16
  17.2 0.7 copy-start.17

commit v2 on v1

--- a/solution.py
+++ b/solution.py
@@ -121,15 +121,28 @@
 
 
 def kernel(
-    feat, gain, head, targ, mask, level,
-    t_hi, t_lo, m_hi, m_lo, s_hi, s_lo, xc, xs, fa_hi, fa_lo, fb_hi, fb_lo, ca, sa,
+    feat_h, gain_h, head_h, targ_h, mask_h, level_h, mats_h, turn_h, twist_h,
     out, loss,
+    feat, gain, head, targ, mask, level, mats, turn, twist,
     normed, tm_hi, tm_lo, s0, s1, r0, r1, y0, y1, z0, z1, u, wt, part1, part2,
-    fsend, frecv, bsend, brecv, lsend, lrecv,
+    load, go, fsend, frecv, bsend, brecv, lsend, lrecv,
 ):
+    pairs = (
+        (feat_h, feat), (gain_h, gain), (mask_h, mask), (mats_h, mats), (head_h, head),
+        (targ_h, targ), (turn_h, turn), (level_h, level), (twist_h, twist),
+    )
+    loads = [pltpu.make_async_copy(src, dst, load.at[i]) for i, (src, dst) in enumerate(pairs)]
+    for copy in loads:
+        copy.start()
+    t_hi, t_lo, m_hi, m_lo, s_hi, s_lo, fa_hi, fb_hi = [mats.at[i] for i in range(8)]
+    fa_lo, fb_lo = mats.at[8, :, pl.ds(0, 128)], mats.at[8, :, pl.ds(128, 128)]
+    xc, xs, ca, sa = turn.at[0], turn.at[1], twist.at[0], twist.at[1]
     me = lax.axis_index("seq")
     mz = lax.rem(me, ZR)
     mq = me // ZR
+    scene = lax.axis_index("scene")
+    late = lax.rem(scene, 2) == 1
+    twin = {"seq": me, "scene": scene + 1 - 2 * lax.rem(scene, 2)}
     sends, recvs, backs, homes = (s0, s1), (r0, r1), (y0, y1), (z0, z1)
 
     barrier = pltpu.get_barrier_semaphore()
@@ -138,12 +151,18 @@
     def _(p):
         pl.semaphore_signal(barrier, inc=1, device_id={"seq": lax.rem(me + p, N)}, device_id_type=MESH)
 
+    pl.semaphore_signal(barrier, inc=1, device_id=twin, device_id_type=MESH)
+    loads[0].wait()
+    loads[1].wait()
+    weight = gain[...].reshape(1, D)
     for row in range(0, TOK, 64):
         values = feat[row : row + 64, :].astype(F32)
         centre = values - jnp.mean(values, axis=-1, keepdims=True)
         spread = jnp.mean(centre * centre, axis=-1, keepdims=True)
-        normed[row : row + 64, :] = (centre * lax.rsqrt(spread + 1e-06) * gain[...]).astype(BF16)
-
+        normed[row : row + 64, :] = (centre * lax.rsqrt(spread + 1e-06) * weight).astype(BF16)
+
+    loads[2].wait()
+    loads[3].wait()
     keep = mask[...].astype(F32)
     tm_hi[...] = (t_hi[...].astype(F32) * keep).astype(BF16)
     tm_lo[...] = (t_lo[...].astype(F32) * keep).astype(BF16)
@@ -167,6 +186,8 @@
 
     mine = pl.ds(pl.multiple_of(me * 8, 8), 8)
 
+    for i in (4, 5, 6):
+        loads[i].wait()
     for h in range(2):
         for g in range(2):
             lo = h * 512 + g * 256
@@ -185,9 +206,16 @@
                     sends[h][r + i : r + i + 1, :] = first[:1, i * 128 : i * 128 + 128]
         recvs[h][mine, :] = sends[h][mine, :]
         if h == 0:
-            pl.semaphore_wait(barrier, N - 1)
+            pl.semaphore_wait(barrier, N)
+
+            @pl.when(late)
+            def _():
+                pl.semaphore_wait(go, 1)
+
         scatter(sends[h], recvs[h], fsend.at[h], frecv.at[h])
 
+    loads[7].wait()
+    loads[8].wait()
     lane = lax.broadcasted_iota(jnp.int32, (128, 128), 1)
     row = lax.broadcasted_iota(jnp.int32, (128, 128), 0)
     k2 = lax.shift_right_logical(lane, 2) & 15
@@ -204,6 +232,13 @@
         for i in range(NBIN):
             value = jnp.where(band == i, level[i].astype(F32), value)
         wt[jb] = value * 0.125
+
+    for h in range(2):
+        await_all(sends[h], fsend.at[h])
+
+    @pl.when(jnp.logical_not(late))
+    def _():
+        pl.semaphore_signal(go, inc=1, device_id=twin, device_id_type=MESH)
 
     def swap(x):
         return pltpu.roll(x, 64, 1) * sign[: x.shape[0]]
@@ -303,27 +338,37 @@
     pltpu.make_async_copy(far, far, lrecv.at[1]).wait()
     loss[0] = jnp.sum(part2[...]) * (1.0 / 33554432.0)
     for h in range(2):
-        await_all(sends[h], fsend.at[h])
         await_all(backs[h], bsend.at[h])
 
 
 def shards(features, norm_gain, pred_weight, target, patch_mask, band_level):
     plain, first = pixel_tables()
     outer, inner, ca, sa = row_tables()
-    tables = [
-        *halves(token_table()), *halves(plain), *halves(first), *pixel_turn(),
-        *doubled(outer), *doubled(inner), ca, sa,
-    ]
-    vmem = pl.BlockSpec(memory_space=pltpu.VMEM)
-    smem = pl.BlockSpec(memory_space=pltpu.SMEM)
+    outer_hi, outer_lo = doubled(outer)
+    inner_hi, inner_lo = doubled(inner)
+    mats = np.stack([
+        *halves(token_table()), *halves(plain), *halves(first), outer_hi, inner_hi,
+        np.concatenate([outer_lo, inner_lo], axis=1),
+    ])
+    tables = [mats, np.stack(pixel_turn()), np.stack([ca, sa])]
+    hbm = pl.BlockSpec(memory_space=pltpu.HBM)
     dma = pltpu.SemaphoreType.DMA
     block = pltpu.VMEM((N * 8, 128), F32)
     grad, loss = pl.pallas_call(
         kernel,
         out_shape=(jax.ShapeDtypeStruct((TOK, PIX), F32), jax.ShapeDtypeStruct((1,), F32)),
-        in_specs=[vmem] * 5 + [smem] + [vmem] * len(tables),
-        out_specs=(vmem, smem),
+        in_specs=[hbm] * (6 + len(tables)),
+        out_specs=(pl.BlockSpec(memory_space=pltpu.VMEM), pl.BlockSpec(memory_space=pltpu.SMEM)),
         scratch_shapes=[
+            pltpu.VMEM((TOK, D), BF16),
+            pltpu.VMEM((D,), F32),
+            pltpu.VMEM((D, PIX), BF16),
+            pltpu.VMEM((TOK, PIX), BF16),
+            pltpu.VMEM((1, TOK), jnp.int32),
+            pltpu.SMEM((NBIN,), jnp.int32),
+            pltpu.VMEM((9, 256, 256), BF16),
+            pltpu.VMEM((2, 128, 128), F32),
+            pltpu.VMEM((2, 16, 128, 128), F32),
             pltpu.VMEM((TOK, D), BF16),
             pltpu.VMEM((TOK, TOK), BF16),
             pltpu.VMEM((TOK, TOK), BF16),
@@ -332,13 +377,15 @@
             pltpu.VMEM((16, 128, 128), F32),
             pltpu.VMEM((ZR * 8, 128), F32),
             pltpu.VMEM((QR * 8, 128), F32),
+            dma((9,)),
+            pltpu.SemaphoreType.REGULAR,
             *[dma((2,))] * 6,
         ],
         compiler_params=pltpu.CompilerParams(
-            collective_id=0, has_side_effects=True, vmem_limit_bytes=48 * 2**20
+            collective_id=0, has_side_effects=True, vmem_limit_bytes=32 * 2**20
         ),
     )(
-        features, norm_gain.reshape(1, D), pred_weight, target, patch_mask.reshape(1, TOK), band_level,
+        features, norm_gain, pred_weight, target, patch_mask.reshape(1, TOK), band_level,
         *[jnp.asarray(table) for table in tables],
     )
     return grad, loss

time: 152 us -> 138 us (0.908); the launches traced: 149 us -> 137 us
  local copies, waits for them, and re-layouts: 18.2 us -> 10.6 us
  Pallas kernels: 129 us -> 124 us
    unnamed x37 -> x19, local copies, waits for them, and re-layouts: 17.5 us -> 10.6 us
    pallas_call x1, Pallas kernels: 129 us -> 124 us  [shards(): pl.pallas_call(kernel, out_shape=(jax.ShapeDtypeStruct((TOK, PIX), F32),...]
where the time goes in v2:
time: 138 us; the launch traced here: 137 us
  Pallas kernels  124 us (90%)
  local copies, waits for them, and re-layouts  10.6 us (8%)
  between operations  2.41 us (2%)
    pallas_call x1, Pallas kernels, shards(): pl.pallas_call(kernel, out_shape=(jax.ShapeDtypeStruct((TOK, PIX), F32),...  124 us
    unnamed x19, local copies, waits for them, and re-layouts  10.6 us

profile of v2, /device:TPU:1, one launch (start us, length us, event | category | flops | bytes accessed | tf_op | source)
XLA Modules:
  0.0 137.2 jit_solution(894144038938936403)
XLA Ops:
  0.6 0.0 copy-start
  0.6 1.7 %copy-done = bf16[1280,1024]{1,0:T(8,128)(2,1)S(1)} copy-done((bf16[1280,1024]{1,0:T(8,128)(2,1)S(1)}, bf16[1280,1024]{1,0:T(8,128)(2,1)}, u32[]{:S(2)}) %copy-start) | copy-done | bytes 2621464
  2.4 0.0 copy-start.1
  2.4 1.6 %copy-done.1 = f32[2,16,128,128]{3,2,1,0:T(8,128)S(1)} copy-done((f32[2,16,128,128]{3,2,1,0:T(8,128)S(1)}, f32[2,16,128,128]{3,2,1,0:T(8,128)}, u32[]{:S(2)}) %copy-start.1) | copy-done | bytes 2097176
  4.0 0.0 copy-start.2
  4.0 1.3 copy-done.2
  5.2 0.0 copy-start.3
  5.2 1.1 copy-done.3
  6.3 0.0 copy-start.4
  6.3 1.0 copy-done.4
  7.4 0.0 copy-start.5
  7.4 0.9 copy-done.5
  8.3 0.0 copy-start.6
  8.3 0.7 copy-done.6
  9.0 0.0 copy-start.7
  9.0 0.7 copy-done.7
  9.6 0.0 copy-start.8
  9.6 0.7 copy-done.8
  10.3 124.2 %shard_map.104 = (f32[256,1024]{1,0:T(8,128)S(1)}, f32[1]{0:T(128)}) custom-call(bf16[256,1280]{1,0:T(8,128)(2,1)S(1)} %copy-done.3, f32[1280]{0:T(1024)S(1)} %copy-done.6, bf16[1280,1024]{1,0:T(8,128)(2,1)S(1)} %copy-done, bf16[256,1024]{1,0:T(8,128)(2,1)S(1)} %copy-done.4, s32[1,256]{1,0:T(1,128)S(1)} %bitcast.1, s32[16]{0:T(128)S(1)} %copy-done.8, ...), custom_call_target="tpu_custom_call" | custom-call | tf_op jit(solution)/shard_map/pallas_call | solution.py:357
  134.5 1.0 copy.13
Async XLA Ops:
  0.6 1.7 %copy-start = (bf16[1280,1024]{1,0:T(8,128)(2,1)S(1)}, bf16[1280,1024]{1,0:T(8,128)(2,1)}, u32[]{:S(2)}) copy-start(bf16[1280,1024]{1,0:T(8,128)(2,1)} %head_h.1) | copy-start | bytes 7864324
  2.4 1.6 %copy-start.1 = (f32[2,16,128,128]{3,2,1,0:T(8,128)S(1)}, f32[2,16,128,128]{3,2,1,0:T(8,128)}, u32[]{:S(2)}) copy-start(f32[2,16,128,128]{3,2,1,0:T(8,128)} %constant.8.clone.twist_h) | copy-start | bytes 6291460
  4.0 1.3 copy-start.2
  5.2 1.1 copy-start.3
  6.3 1.0 copy-start.4
  7.4 0.9 copy-start.5
  8.3 0.7 copy-start.6
  9.0 0.7 copy-start.7
  9.6 0.7 copy-start.8

commit v3 on v2

--- a/solution.py
+++ b/solution.py
@@ -122,10 +122,10 @@
 
 def kernel(
     feat_h, gain_h, head_h, targ_h, mask_h, level_h, mats_h, turn_h, twist_h,
-    out, loss,
+    out_h, loss,
     feat, gain, head, targ, mask, level, mats, turn, twist,
-    normed, tm_hi, tm_lo, s0, s1, r0, r1, y0, y1, z0, z1, u, wt, part1, part2,
-    load, go, fsend, frecv, bsend, brecv, lsend, lrecv,
+    normed, tm_hi, tm_lo, s0, s1, r0, r1, y0, y1, z0, z1, u, wt, part1, part2, out,
+    load, save, go, fsend, frecv, bsend, brecv, lsend, lrecv,
 ):
     pairs = (
         (feat_h, feat), (gain_h, gain), (mask_h, mask), (mats_h, mats), (head_h, head),
@@ -233,12 +233,13 @@
             value = jnp.where(band == i, level[i].astype(F32), value)
         wt[jb] = value * 0.125
 
-    for h in range(2):
-        await_all(sends[h], fsend.at[h])
+    await_all(sends[0], fsend.at[0])
 
     @pl.when(jnp.logical_not(late))
     def _():
         pl.semaphore_signal(go, inc=1, device_id=twin, device_id_type=MESH)
+
+    await_all(sends[1], fsend.at[1])
 
     def swap(x):
         return pltpu.roll(x, 64, 1) * sign[: x.shape[0]]
@@ -255,7 +256,7 @@
                 u[h * 8 + r + i] = (c * p - s * q) + swap(c * q + s * p)
 
     def middle(jb, acc):
-        at = [pl.ds(pl.multiple_of(jb * 16 + i * 8, 8), 8) for i in range(2)]
+        at = [pl.ds(jb * 16 + i * 8, 8) for i in range(2)]
         x = jnp.concatenate([u[:, at[i], :].reshape(128, 128) for i in range(2)], axis=1)
         pq = stacked(fb_hi[...], fb_lo[...], x)
         vs = []
@@ -272,7 +273,9 @@
             u[:, at[i], :] = ((c * p - s * q) - swap(c * q + s * p)).reshape(16, 8, 128)
         return acc
 
-    acc = lax.fori_loop(0, 8, middle, jnp.zeros((8, 128), F32))
+    acc = jnp.zeros((8, 128), F32)
+    for jb in range(8):
+        acc = middle(jb, acc)
 
     part1[pl.ds(pl.multiple_of(mz * 8, 8), 8), :] = acc
 
@@ -314,6 +317,7 @@
             device_id_type=MESH,
         ).start()
 
+    saves = []
     for h in range(2):
         await_all(homes[h], brecv.at[h])
         for g in range(2):
@@ -332,6 +336,12 @@
                 blocks.append(jnp.concatenate([a * xc[...] + b * xs[...], b * xc[...] - a * xs[...]], axis=0))
             grad = left(tm_hi[...], tm_lo[...], jnp.concatenate(blocks, axis=1), ((0,), (0,)))
             out[:, lo : lo + 256] = grad * 2.0
+            saves.append(
+                pltpu.make_async_copy(
+                    out.at[:, pl.ds(lo, 256)], out_h.at[:, pl.ds(lo, 256)], save.at[h * 2 + g]
+                )
+            )
+            saves[-1].start()
 
     far = part2.at[pl.ds(0, (QR - 1) * 8)]
     pltpu.make_async_copy(far, far, lsend.at[1]).wait()
@@ -339,6 +349,8 @@
     loss[0] = jnp.sum(part2[...]) * (1.0 / 33554432.0)
     for h in range(2):
         await_all(backs[h], bsend.at[h])
+    for copy in saves:
+        copy.wait()
 
 
 def shards(features, norm_gain, pred_weight, target, patch_mask, band_level):
@@ -358,7 +370,7 @@
         kernel,
         out_shape=(jax.ShapeDtypeStruct((TOK, PIX), F32), jax.ShapeDtypeStruct((1,), F32)),
         in_specs=[hbm] * (6 + len(tables)),
-        out_specs=(pl.BlockSpec(memory_space=pltpu.VMEM), pl.BlockSpec(memory_space=pltpu.SMEM)),
+        out_specs=(hbm, pl.BlockSpec(memory_space=pltpu.SMEM)),
         scratch_shapes=[
             pltpu.VMEM((TOK, D), BF16),
             pltpu.VMEM((D,), F32),
@@ -377,12 +389,14 @@
             pltpu.VMEM((16, 128, 128), F32),
             pltpu.VMEM((ZR * 8, 128), F32),
             pltpu.VMEM((QR * 8, 128), F32),
+            pltpu.VMEM((TOK, PIX), F32),
             dma((9,)),
+            dma((4,)),
             pltpu.SemaphoreType.REGULAR,
             *[dma((2,))] * 6,
         ],
         compiler_params=pltpu.CompilerParams(
-            collective_id=0, has_side_effects=True, vmem_limit_bytes=32 * 2**20
+            collective_id=0, has_side_effects=True, vmem_limit_bytes=60 * 2**20
         ),
     )(
         features, norm_gain, pred_weight, target, patch_mask.reshape(1, TOK), band_level,

time: 138 us -> 126 us (0.913)
  local copies, waits for them, and re-layouts: 10.6 us -> 2.31 us
  Pallas kernels: 124 us -> 121 us
    unnamed x19 -> x1, local copies, waits for them, and re-layouts: 10.6 us -> 2.31 us
    pallas_call x1, Pallas kernels: 124 us -> 121 us  [shards(): pl.pallas_call(kernel, out_shape=(jax.ShapeDtypeStruct((TOK, PIX), F32),...]
where the time goes in v3:
time: 126 us
  Pallas kernels  121 us (96%)
  between operations  2.33 us (2%)
  local copies, waits for them, and re-layouts  2.31 us (2%)
    pallas_call x1, Pallas kernels, shards(): pl.pallas_call(kernel, out_shape=(jax.ShapeDtypeStruct((TOK, PIX), F32),...  121 us

profile of v3, /device:TPU:1, one launch (start us, length us, event | category | flops | bytes accessed | tf_op | source)
XLA Modules:
  0.0 125.9 jit_solution(15247356600594026192)
XLA Ops:
  0.6 121.3 %shard_map.104 = (f32[256,1024]{1,0:T(8,128)}, f32[1]{0:T(128)}) custom-call(bf16[256,1280]{1,0:T(8,128)(2,1)} %feat_h.1, f32[1280]{0:T(1024)} %gain_h.1, bf16[1280,1024]{1,0:T(8,128)(2,1)} %head_h.1, bf16[256,1024]{1,0:T(8,128)(2,1)} %targ_h.1, s32[1,256]{1,0:T(1,128)} %bitcast.1, s32[16]{0:T(128)} %level_h.1, bf16[9,256,256]{2,1,0:T(8,128)(2,1)} %constant.6.clone.mats_h, ...), custom_call_target="tpu_custom_call" | custom-call | tf_op jit(solution)/shard_map/pallas_call | solution.py:369
  121.9 2.3 %copy.13 = f32[256,1024]{1,0:T(8,128)} copy(f32[256,1024]{1,0:T(8,128)} %get-tuple-element.4) | data formatting | bytes 2097152

commit v4 on v3

--- a/solution.py
+++ b/solution.py
@@ -124,7 +124,7 @@
     feat_h, gain_h, head_h, targ_h, mask_h, level_h, mats_h, turn_h, twist_h,
     out_h, loss,
     feat, gain, head, targ, mask, level, mats, turn, twist,
-    normed, tm_hi, tm_lo, s0, s1, r0, r1, y0, y1, z0, z1, u, wt, part1, part2, out,
+    normed, tm_hi, tm_lo, s0, s1, r0, r1, y0, y1, z0, z1, u, wt, part1, part2, out, own,
     load, save, go, fsend, frecv, bsend, brecv, lsend, lrecv,
 ):
     pairs = (
@@ -167,24 +167,56 @@
     tm_hi[...] = (t_hi[...].astype(F32) * keep).astype(BF16)
     tm_lo[...] = (t_lo[...].astype(F32) * keep).astype(BF16)
 
-    def scatter(src, dst, send, recv):
+    def scatter(src, dst, send, recv, rows):
         @pl.loop(1, N)
         def _(p):
             t = lax.rem(me + p, N)
             pltpu.make_async_remote_copy(
-                src_ref=src.at[pl.ds(pl.multiple_of(t * 8, 8), 8)],
-                dst_ref=dst.at[pl.ds(pl.multiple_of(me * 8, 8), 8)],
+                src_ref=src.at[pl.ds(pl.multiple_of(t * 8, 8), rows)],
+                dst_ref=dst.at[pl.ds(pl.multiple_of(me * 8, 8), rows)],
                 send_sem=send,
                 recv_sem=recv,
                 device_id={"seq": t},
                 device_id_type=MESH,
             ).start()
 
-    def await_all(ref, sem):
-        whole = ref.at[pl.ds(0, (N - 1) * 8)]
+    def await_all(ref, sem, rows):
+        whole = ref.at[pl.ds(0, (N - 1) * rows)]
         pltpu.make_async_copy(whole, whole, sem).wait()
 
     mine = pl.ds(pl.multiple_of(me * 8, 8), 8)
+    lane = lax.broadcasted_iota(jnp.int32, (128, 128), 1)
+    row = lax.broadcasted_iota(jnp.int32, (128, 128), 0)
+    k2 = lax.shift_right_logical(lane, 2) & 15
+    top_band = k2 == 8
+
+    def spare(r, drop):
+        group = r - (drop == 0)
+        group = group + (group > 7)
+        return group, 32 - 4 * group
+
+    def packed(x, dropped, r, drop):
+        return jnp.where(top_band, pltpu.roll(dropped, spare(r, drop)[1] % 128, 1), x)
+
+    def unpacked(blocks, drop):
+        dropped = jnp.zeros((128, 128), F32)
+        for r in range(16):
+            if r != drop:
+                group, shift = spare(r, drop)
+                moved = pltpu.roll(rows_of(blocks, r, drop), -shift % 128, 1)
+                dropped = jnp.where(k2 == group, moved, dropped)
+        return dropped
+
+    def rows_of(blocks, r, drop):
+        return blocks[r // 8][pl.ds(r % 8 - (drop == 0 and r < 8), 128, stride=8), :]
+
+    def put_rows(blocks, r, x, drop):
+        blocks[r // 8][pl.ds(r % 8 - (drop == 0 and r < 8), 128, stride=8), :] = x
+
+    def with_first(spec, first):
+        top = lax.broadcasted_iota(jnp.int32, (8, 256), 0)
+        head8 = jnp.where(top == 0, jnp.broadcast_to(first[:1], (8, 256)), spec[:8])
+        return jnp.concatenate([head8, spec[8:]], axis=0)
 
     for i in (4, 5, 6):
         loads[i].wait()
@@ -194,16 +226,19 @@
             error = mm(normed[...], head[:, lo : lo + 256]) - targ[:, lo : lo + 256].astype(F32)
             ab = left(tm_hi[...], tm_lo[...], error)
             for pr in range(2):
-                r = g * 4 + pr * 2
+                r = h * 8 + g * 4 + pr * 2
                 a = ab[:128, pr * 128 : pr * 128 + 128]
                 b = ab[128:, pr * 128 : pr * 128 + 128]
                 a, b = a * xc[...] - b * xs[...], b * xc[...] + a * xs[...]
                 both = jnp.concatenate([a, b], axis=1)
-                spec = times(both, m_hi[...], m_lo[...])
-                first = times(both[:8], s_hi[...], s_lo[...])
+                spec = with_first(times(both, m_hi[...], m_lo[...]), times(both[:8], s_hi[...], s_lo[...]))
                 for i in range(2):
-                    sends[h][pl.ds(r + i, 128, stride=8), :] = spec[:, i * 128 : i * 128 + 128]
-                    sends[h][r + i : r + i + 1, :] = first[:1, i * 128 : i * 128 + 128]
+                    part = spec[:, i * 128 : i * 128 + 128]
+                    own[r + i] = part
+                    if r + i == 0:
+                        zeroth = part
+                    else:
+                        put_rows(sends, r + i, packed(part, zeroth, r + i, 0), 0)
         recvs[h][mine, :] = sends[h][mine, :]
         if h == 0:
             pl.semaphore_wait(barrier, N)
@@ -212,13 +247,10 @@
             def _():
                 pl.semaphore_wait(go, 1)
 
-        scatter(sends[h], recvs[h], fsend.at[h], frecv.at[h])
+        scatter(sends[h], recvs[h], fsend.at[h], frecv.at[h], 7 + h)
 
     loads[7].wait()
     loads[8].wait()
-    lane = lax.broadcasted_iota(jnp.int32, (128, 128), 1)
-    row = lax.broadcasted_iota(jnp.int32, (128, 128), 0)
-    k2 = lax.shift_right_logical(lane, 2) & 15
     band_x = jnp.where(k2 < 8, 2 * k2, 31 - 2 * k2)
     band_x = jnp.where((lane & 1) + k2 * 2 + me * 64 == 1, NBIN - 1, band_x)
     sign = jnp.where(lane < 64, 1.0, -1.0).astype(F32)
@@ -231,29 +263,42 @@
         value = jnp.zeros((128, 128), F32)
         for i in range(NBIN):
             value = jnp.where(band == i, level[i].astype(F32), value)
-        wt[jb] = value * 0.125
-
-    await_all(sends[0], fsend.at[0])
+        wt[jb] = jnp.where(top_band, 0.0, value * 0.125)
+
+    level_top = level[NBIN - 1].astype(F32) * 0.125
+    acc = jnp.zeros((8, 128), F32)
+    for r in range(16):
+        part = jnp.where(top_band, own[r], 0.0)
+        scaled = level_top * part
+        own[r] = scaled
+        acc = acc + jnp.sum((scaled * part).reshape(16, 8, 128), axis=0)
+
+    await_all(sends[0], fsend.at[0], 7)
 
     @pl.when(jnp.logical_not(late))
     def _():
         pl.semaphore_signal(go, inc=1, device_id=twin, device_id_type=MESH)
 
-    await_all(sends[1], fsend.at[1])
+    await_all(sends[1], fsend.at[1], 8)
 
     def swap(x):
         return pltpu.roll(x, 64, 1) * sign[: x.shape[0]]
 
-    for h in range(2):
-        await_all(recvs[h], frecv.at[h])
-        for r in range(0, 8, 2):
-            x = jnp.concatenate([recvs[h][pl.ds(r + i, 128, stride=8), :] for i in range(2)], axis=1)
-            pq = stacked(fa_hi[...], fa_lo[...], x)
-            for i in range(2):
-                p = pq[:128, i * 128 : i * 128 + 128]
-                q = pq[128:, i * 128 : i * 128 + 128]
-                c, s = ca[h * 8 + r + i], sa[h * 8 + r + i]
-                u[h * 8 + r + i] = (c * p - s * q) + swap(c * q + s * p)
+    def outward(r, xs2):
+        pq = stacked(fa_hi[...], fa_lo[...], jnp.concatenate(xs2, axis=1))
+        for i in range(len(xs2)):
+            p = pq[:128, i * 128 : i * 128 + 128]
+            q = pq[128:, i * 128 : i * 128 + 128]
+            c, s = ca[r + i], sa[r + i]
+            u[r + i] = (c * p - s * q) + swap(c * q + s * p)
+
+    await_all(recvs[0], frecv.at[0], 7)
+    for r in range(2, 8, 2):
+        outward(r, [rows_of(recvs, r, 0), rows_of(recvs, r + 1, 0)])
+    await_all(recvs[1], frecv.at[1], 8)
+    outward(0, [unpacked(recvs, 0), rows_of(recvs, 1, 0)])
+    for r in range(8, 16, 2):
+        outward(r, [rows_of(recvs, r, 0), rows_of(recvs, r + 1, 0)])
 
     def middle(jb, acc):
         at = [pl.ds(jb * 16 + i * 8, 8) for i in range(2)]
@@ -273,7 +318,6 @@
             u[:, at[i], :] = ((c * p - s * q) - swap(c * q + s * p)).reshape(16, 8, 128)
         return acc
 
-    acc = jnp.zeros((8, 128), F32)
     for jb in range(8):
         acc = middle(jb, acc)
 
@@ -290,16 +334,23 @@
             device_id_type=MESH,
         ).start()
 
-    for h in range(2):
-        for r in range(0, 8, 2):
-            x = jnp.concatenate([u[h * 8 + r + i] for i in range(2)], axis=1)
-            pq = stacked(fa_hi[...], fa_lo[...], x)
-            for i in range(2):
-                p = pq[:128, i * 128 : i * 128 + 128]
-                q = pq[128:, i * 128 : i * 128 + 128]
-                backs[h][pl.ds(r + i, 128, stride=8), :] = p - swap(q)
-        homes[h][mine, :] = backs[h][mine, :]
-        scatter(backs[h], homes[h], bsend.at[h], brecv.at[h])
+    last = None
+    for r in (14, 0, 2, 4, 6, 8, 10, 12):
+        pq = stacked(fa_hi[...], fa_lo[...], jnp.concatenate([u[r], u[r + 1]], axis=1))
+        columns = []
+        for i in range(2):
+            p = pq[:128, i * 128 : i * 128 + 128]
+            q = pq[128:, i * 128 : i * 128 + 128]
+            columns.append(p - swap(q))
+        if r == 14:
+            last = columns[1]
+        for i in range(2):
+            if r + i != 15:
+                put_rows(backs, r + i, packed(columns[i], last, r + i, 15), 15)
+        if r == 6 or r == 12:
+            h = r // 8
+            homes[h][mine, :] = backs[h][mine, :]
+            scatter(backs[h], homes[h], bsend.at[h], brecv.at[h], 8 - h)
 
     near = part1.at[pl.ds(0, (ZR - 1) * 8)]
     pltpu.make_async_copy(near, near, lsend.at[0]).wait()
@@ -318,37 +369,38 @@
         ).start()
 
     saves = []
+
+    def home_row(r):
+        return jnp.where(top_band, own[r], unpacked(homes, 15) if r == 15 else rows_of(homes, r, 15))
+
+    def inward(g):
+        blocks = []
+        for pr in range(2):
+            r = g * 4 + pr * 2
+            x = jnp.concatenate([home_row(r), home_row(r + 1)], axis=1)
+            flip = ((1,), (1,))
+            spec = with_first(times(x, m_hi[...], m_lo[...], flip), times(x[:8], s_hi[...], s_lo[...], flip))
+            a, b = spec[:, :128], spec[:, 128:]
+            blocks.append(jnp.concatenate([a * xc[...] + b * xs[...], b * xc[...] - a * xs[...]], axis=0))
+        grad = left(tm_hi[...], tm_lo[...], jnp.concatenate(blocks, axis=1), ((0,), (0,)))
+        lo = g * 256
+        out[:, lo : lo + 256] = grad
+        saves.append(
+            pltpu.make_async_copy(out.at[:, pl.ds(lo, 256)], out_h.at[:, pl.ds(lo, 256)], save.at[g])
+        )
+        saves[-1].start()
+
     for h in range(2):
-        await_all(homes[h], brecv.at[h])
+        await_all(homes[h], brecv.at[h], 8 - h)
         for g in range(2):
-            lo = h * 512 + g * 256
-            blocks = []
-            for pr in range(2):
-                r = g * 4 + pr * 2
-                x = jnp.concatenate([homes[h][pl.ds(r + i, 128, stride=8), :] for i in range(2)], axis=1)
-                flip = ((1,), (1,))
-                spec = times(x, m_hi[...], m_lo[...], flip)
-                first = times(x[:8], s_hi[...], s_lo[...], flip)
-                top = lax.broadcasted_iota(jnp.int32, (8, 256), 0)
-                head8 = jnp.where(top == 0, jnp.broadcast_to(first[:1], (8, 256)), spec[:8])
-                spec = jnp.concatenate([head8, spec[8:]], axis=0)
-                a, b = spec[:, :128], spec[:, 128:]
-                blocks.append(jnp.concatenate([a * xc[...] + b * xs[...], b * xc[...] - a * xs[...]], axis=0))
-            grad = left(tm_hi[...], tm_lo[...], jnp.concatenate(blocks, axis=1), ((0,), (0,)))
-            out[:, lo : lo + 256] = grad * 2.0
-            saves.append(
-                pltpu.make_async_copy(
-                    out.at[:, pl.ds(lo, 256)], out_h.at[:, pl.ds(lo, 256)], save.at[h * 2 + g]
-                )
-            )
-            saves[-1].start()
+            inward(h * 2 + g)
 
     far = part2.at[pl.ds(0, (QR - 1) * 8)]
     pltpu.make_async_copy(far, far, lsend.at[1]).wait()
     pltpu.make_async_copy(far, far, lrecv.at[1]).wait()
-    loss[0] = jnp.sum(part2[...]) * (1.0 / 33554432.0)
+    loss[0] = jnp.sum(part2[...])
     for h in range(2):
-        await_all(backs[h], bsend.at[h])
+        await_all(backs[h], bsend.at[h], 8 - h)
     for copy in saves:
         copy.wait()
 
@@ -390,6 +442,7 @@
             pltpu.VMEM((ZR * 8, 128), F32),
             pltpu.VMEM((QR * 8, 128), F32),
             pltpu.VMEM((TOK, PIX), F32),
+            pltpu.VMEM((16, 128, 128), F32),
             dma((9,)),
             dma((4,)),
             pltpu.SemaphoreType.REGULAR,
@@ -402,7 +455,7 @@
         features, norm_gain, pred_weight, target, patch_mask.reshape(1, TOK), band_level,
         *[jnp.asarray(table) for table in tables],
     )
-    return grad, loss
+    return grad * 2.0, loss * (1.0 / 33554432.0)
 
 
 def solution(mesh):

time: 126 us -> 122 us (0.968)
  Pallas kernels: 121 us -> 117 us
  other arithmetic: 0 us -> 2.31 us
  local copies, waits for them, and re-layouts: 2.31 us -> 0 us
    pallas_call x1, Pallas kernels: 121 us -> 117 us  [shards(): pl.pallas_call(kernel, out_shape=(jax.ShapeDtypeStruct((TOK, PIX), F32),...]
    mul x0 -> x1, other arithmetic: none -> 2.31 us  [shards(): return (grad * 2.0, loss * (1.0 / 33554432.0))]
    unnamed x1 -> x0, local copies, waits for them, and re-layouts: 2.31 us -> none
where the time goes in v4:
time: 122 us
  Pallas kernels  117 us (96%)
  between operations  2.33 us (2%)
  other arithmetic  2.31 us (2%)
    pallas_call x1, Pallas kernels, shards(): pl.pallas_call(kernel, out_shape=(jax.ShapeDtypeStruct((TOK, PIX), F32),...  117 us

profile of v4, /device:TPU:1, one launch (start us, length us, event | category | flops | bytes accessed | tf_op | source)
XLA Modules:
  0.0 122.0 jit_solution(10967865713671977992)
XLA Ops:
  0.6 117.4 %shard_map.104 = (f32[256,1024]{1,0:T(8,128)}, f32[1]{0:T(128)}) custom-call(bf16[256,1280]{1,0:T(8,128)(2,1)} %feat_h.1, f32[1280]{0:T(1024)} %gain_h.1, bf16[1280,1024]{1,0:T(8,128)(2,1)} %head_h.1, bf16[256,1024]{1,0:T(8,128)(2,1)} %targ_h.1, s32[1,256]{1,0:T(1,128)} %bitcast.1, s32[16]{0:T(128)} %level_h.1, bf16[9,256,256]{2,1,0:T(8,128)(2,1)} %constant.10.clone.mats_h, ...), custom_call_target="tpu_custom_call" | custom-call | tf_op jit(solution)/shard_map/pallas_call | solution.py:421
  118.6 2.3 %broadcast_multiply_fusion = f32[256,1024]{1,0:T(8,128)} fusion(f32[256,1024]{1,0:T(8,128)} %get-tuple-element.4), kind=kLoop, calls=%fused_computation | loop fusion | flops 262144 | bytes 2097152 | tf_op jit(solution)/shard_map/mul | solution.py:458

commit v5 on v4

--- a/solution.py
+++ b/solution.py
@@ -167,10 +167,15 @@
     tm_hi[...] = (t_hi[...].astype(F32) * keep).astype(BF16)
     tm_lo[...] = (t_lo[...].astype(F32) * keep).astype(BF16)
 
-    def scatter(src, dst, send, recv, rows):
+    def scatter(src, dst, send, recv, rows, by_z=False):
         @pl.loop(1, N)
         def _(p):
-            t = lax.rem(me + p, N)
+            if by_z:
+                step = p - 1
+                step = step + (step >= mz * QR)
+                t = lax.rem(mq + lax.rem(step, QR), QR) * ZR + step // QR
+            else:
+                t = lax.rem(me + p, N)
             pltpu.make_async_remote_copy(
                 src_ref=src.at[pl.ds(pl.multiple_of(t * 8, 8), rows)],
                 dst_ref=dst.at[pl.ds(pl.multiple_of(me * 8, 8), rows)],
@@ -350,7 +355,7 @@
         if r == 6 or r == 12:
             h = r // 8
             homes[h][mine, :] = backs[h][mine, :]
-            scatter(backs[h], homes[h], bsend.at[h], brecv.at[h], 8 - h)
+            scatter(backs[h], homes[h], bsend.at[h], brecv.at[h], 8 - h, h == 1)
 
     near = part1.at[pl.ds(0, (ZR - 1) * 8)]
     pltpu.make_async_copy(near, near, lsend.at[0]).wait()

time: 122 us -> 118 us (0.967); the launches traced: 122 us -> 116 us
  Pallas kernels: 117 us -> 111 us
    pallas_call x1, Pallas kernels: 117 us -> 111 us  [shards(): pl.pallas_call(kernel, out_shape=(jax.ShapeDtypeStruct((TOK, PIX), F32),...]
where the time goes in v5:
time: 118 us; the launch traced here: 116 us
  Pallas kernels  111 us (94%)
  between operations  2.33 us (2%)
  other arithmetic  2.31 us (2%)
    pallas_call x1, Pallas kernels, shards(): pl.pallas_call(kernel, out_shape=(jax.ShapeDtypeStruct((TOK, PIX), F32),...  111 us

profile of v5, /device:TPU:1, one launch (start us, length us, event | category | flops | bytes accessed | tf_op | source)
XLA Modules:
  0.0 115.9 jit_solution(12355385989767392868)
XLA Ops:
  0.6 111.3 %shard_map.104 = (f32[256,1024]{1,0:T(8,128)}, f32[1]{0:T(128)}) custom-call(bf16[256,1280]{1,0:T(8,128)(2,1)} %feat_h.1, f32[1280]{0:T(1024)} %gain_h.1, bf16[1280,1024]{1,0:T(8,128)(2,1)} %head_h.1, bf16[256,1024]{1,0:T(8,128)(2,1)} %targ_h.1, s32[1,256]{1,0:T(1,128)} %bitcast.1, s32[16]{0:T(128)} %level_h.1, bf16[9,256,256]{2,1,0:T(8,128)(2,1)} %constant.10.clone.mats_h, ...), custom_call_target="tpu_custom_call" | custom-call | tf_op jit(solution)/shard_map/pallas_call | solution.py:426
  112.5 2.3 %broadcast_multiply_fusion = f32[256,1024]{1,0:T(8,128)} fusion(f32[256,1024]{1,0:T(8,128)} %get-tuple-element.4), kind=kLoop, calls=%fused_computation | loop fusion | flops 262144 | bytes 2097152 | tf_op jit(solution)/shard_map/mul | solution.py:463
